TPU v7x, 32 devices: a whole 2x2x4 slice. The times are simulated.
32 devices in a mesh: section: 4 (over z), expert: 8 (over y, x, core).
Axes of the slice: x: 2, y: 2, z: 4, core: 2. Of those that a mesh axis runs over, the one named last changes fastest.
Arguments:
- activations: bfloat16 [4, 1024, 2048], P('section', 'expert'), may hold values from -6 to 6
- gradients: bfloat16 [4, 1024, 2048], P('section', 'expert'), may hold values from -6 to 6
- stashed: bfloat16 [4, 1024, 2048], P('section', 'expert'), may hold values from -6 to 6
- norm_gain: bfloat16 [4, 2048], P('section'), may hold values from 0.5 to 1.5
- router: bfloat16 [4, 2048, 8], P('section'), may hold values from -0.125 to 0.125
- gate_weight: bfloat16 [4, 8, 2048, 768], P('section', 'expert'), may hold values from -0.125 to 0.125
- up_weight: bfloat16 [4, 8, 2048, 768], P('section', 'expert'), may hold values from -0.125 to 0.125
- down_weight: bfloat16 [4, 8, 768, 2048], P('section', 'expert'), may hold values from -0.21875 to 0.21875
- routes_forward: int32 [4, 1024, 2], P('section', 'expert'), may hold values from 0 to 7, all different within a row; in each aligned block of 128 rows (0 to 127, 128 to 255, ..., all dimensions but the last counted through in order) at most 48 rows name the same one
- routes_backward: int32 [4, 1024, 2], P('section', 'expert'), may hold values from 0 to 7, all different within a row; in each aligned block of 128 rows (0 to 127, 128 to 255, ..., all dimensions but the last counted through in order) at most 48 rows name the same one
Outputs:
- layer_out: bfloat16 [4, 1024, 2048], P('section', 'expert')
- input_grad: bfloat16 [4, 1024, 2048], P('section', 'expert')
Inputs may be any that keep to these rules, and one draw needn't show every extreme that they name: `routes_forward`: each token names 2 different experts. In each aligned block of 128 tokens (one index of expert's tokens of one section) no expert is named by more than 48 tokens, a bound that some block reaches. `routes_backward`: each token names 2 different experts. In each aligned block of 128 tokens (one index of expert's tokens of one section) no expert is named by more than 48 tokens, a bound that some block reaches.
All inputs are finite; a program needn't handle non-finite values.
Results may differ from a plain program's by a relative error of at most 0.0059.
Values may be sent and summed in bfloat16 or wider, within the bound.
A program may use at most 128 MiB of HBM per device.

v0:
```python
import jax
import jax.numpy as jnp
from jax import lax
from jax.sharding import PartitionSpec as P

NORM_EPS = 1e-06


def passed_along(value, axis, steps):
    count = lax.axis_size(axis)
    pairs = [(source, (source + steps) % count) for source in range(count)]
    return lax.ppermute(value, axis, pairs)


def normalize(tokens, gain_row):
    values = tokens.astype(jnp.float32)
    inverse = lax.rsqrt(jnp.mean(values * values, axis=-1, keepdims=True) + NORM_EPS)
    normed = (values * inverse * gain_row.astype(jnp.float32)).astype(jnp.bfloat16)
    return (normed, inverse)


def route_weights(normed, router_mat, routes):
    logits = jnp.dot(normed, router_mat, preferred_element_type=jnp.float32)
    columns = jnp.arange(router_mat.shape[1], dtype=jnp.int32)
    matches = (routes[:, :, None] == columns[None, None, :]).astype(jnp.float32)
    picked = jnp.sum(matches * logits[:, None, :], axis=2)
    sigmoids = jax.nn.sigmoid(picked)
    totals = jnp.sum(sigmoids, axis=1, keepdims=True)
    return (sigmoids / totals, sigmoids, totals, matches)


def slot_positions(routes, expert_count, capacity):
    columns = jnp.arange(expert_count, dtype=jnp.int32)
    matches = (routes[:, :, None] == columns[None, None, :]).astype(jnp.int32)
    per_row = jnp.sum(matches, axis=1)
    earlier = jnp.cumsum(per_row, axis=0) - per_row
    slots = jnp.sum(matches * earlier[:, None, :], axis=2)
    return routes * capacity + slots


def dispatch_table(position, scales, slot_count):
    targets = jnp.arange(slot_count, dtype=jnp.int32)
    matches = position[None, :, :] == targets[:, None, None]
    return jnp.sum(jnp.where(matches, scales[None, :, :], 0.0), axis=2).astype(jnp.bfloat16)


def expert_forward(slot_rows, gate_mat, up_mat, down_mat):
    gate = jnp.dot(slot_rows, gate_mat, preferred_element_type=jnp.float32)
    upper = jnp.dot(slot_rows, up_mat, preferred_element_type=jnp.float32)
    hidden = (jax.nn.silu(gate) * upper).astype(jnp.bfloat16)
    result = jnp.dot(hidden, down_mat, preferred_element_type=jnp.float32).astype(jnp.bfloat16)
    return (result, gate, upper)


def expert_backward(slot_rows, slot_grad, gate_mat, up_mat, down_mat):
    result, gate, upper = expert_forward(slot_rows, gate_mat, up_mat, down_mat)
    dims = (((1,), (1,)), ((), ()))
    grad_hidden = lax.dot_general(slot_grad, down_mat, dims, preferred_element_type=jnp.float32)
    sigmoid_gate = jax.nn.sigmoid(gate)
    grad_up = (grad_hidden * gate * sigmoid_gate).astype(jnp.bfloat16)
    grad_gate = (grad_hidden * upper * sigmoid_gate * (1.0 + gate * (1.0 - sigmoid_gate))).astype(
        jnp.bfloat16
    )
    row_grad = lax.dot_general(grad_gate, gate_mat, dims, preferred_element_type=jnp.float32)
    row_grad = row_grad + lax.dot_general(grad_up, up_mat, dims, preferred_element_type=jnp.float32)
    return (result, row_grad.astype(jnp.bfloat16))


def router_backward(scores, weights, sigmoids, totals, matches, router_mat):
    mixed_score = jnp.sum(weights * scores, axis=1, keepdims=True)
    grad_pick = (scores - mixed_score) / totals * sigmoids * (1.0 - sigmoids)
    grad_logits = jnp.sum(grad_pick[:, :, None] * matches, axis=1)
    return jnp.dot(grad_logits, router_mat.astype(jnp.float32).T, precision=lax.Precision.HIGHEST)


def norm_backward(tokens, inverse, gain_row, grad_normed):
    values = tokens.astype(jnp.float32)
    grad_pre = grad_normed * gain_row.astype(jnp.float32)
    cubed = inverse * inverse * inverse
    return inverse * grad_pre - values * cubed * jnp.mean(grad_pre * values, axis=-1, keepdims=True)


def body(
    activations,
    gradients,
    stashed,
    norm_gain,
    router,
    gate_weight,
    up_weight,
    down_weight,
    routes_forward,
    routes_backward,
):
    arrived = passed_along(activations, "section", 1)[0]
    cotangent = passed_along(gradients, "section", -1)[0]
    owners = lax.axis_size("expert")
    per_source, model_width = arrived.shape
    top_count = routes_forward.shape[2]
    capacity = 3 * per_source * top_count // (2 * owners)
    slot_count = owners * capacity
    gate_mat = gate_weight[0, 0]
    up_mat = up_weight[0, 0]
    down_mat = down_weight[0, 0]
    gain_row = norm_gain[0]
    router_mat = router[0]
    stored = stashed[0]
    normed_f, inverse_f = normalize(arrived, gain_row)
    weights_f, sig_f, tot_f, match_f = route_weights(normed_f, router_mat, routes_forward[0])
    position_f = slot_positions(routes_forward[0], owners, capacity)
    unit_scales = jnp.ones(position_f.shape, jnp.float32)
    table_f = dispatch_table(position_f, unit_scales, slot_count)
    buffer_f = jnp.dot(table_f, normed_f, preferred_element_type=jnp.float32).astype(jnp.bfloat16)
    buffer_f = buffer_f.reshape(owners, capacity, model_width)
    normed_b, inverse_b = normalize(stored, gain_row)
    weights_b, sig_b, tot_b, match_b = route_weights(normed_b, router_mat, routes_backward[0])
    position_b = slot_positions(routes_backward[0], owners, capacity)
    table_b = dispatch_table(position_b, unit_scales, slot_count)
    buffer_b = jnp.dot(table_b, normed_b, preferred_element_type=jnp.float32).astype(jnp.bfloat16)
    buffer_b = buffer_b.reshape(owners, capacity, model_width)
    scale_round = lax.optimization_barrier(weights_b.astype(jnp.bfloat16)).astype(jnp.float32)
    scaled_table = dispatch_table(position_b, scale_round, slot_count)
    grad_buffer = jnp.dot(table_b, cotangent, preferred_element_type=jnp.float32).astype(
        jnp.bfloat16
    )
    grad_buffer = grad_buffer.reshape(owners, capacity, model_width)
    scale_slots = (
        jnp.sum(scaled_table.astype(jnp.float32), axis=1)
        .astype(jnp.bfloat16)
        .reshape(owners, capacity)
    )
    front_rows = lax.all_to_all(buffer_f, "expert", split_axis=0, concat_axis=0, tiled=True)
    back_rows = lax.all_to_all(buffer_b, "expert", split_axis=0, concat_axis=0, tiled=True)
    grad_rows = lax.all_to_all(grad_buffer, "expert", split_axis=0, concat_axis=0, tiled=True)
    scale_part = lax.all_to_all(scale_slots, "expert", split_axis=0, concat_axis=0, tiled=True)
    block_shape = front_rows.shape
    front_out = expert_forward(front_rows.reshape(-1, model_width), gate_mat, up_mat, down_mat)[0]
    slot_grad = (scale_part.astype(jnp.float32)[:, :, None] * grad_rows.astype(jnp.float32)).astype(
        jnp.bfloat16
    )
    back_out, back_grad = expert_backward(
        back_rows.reshape(-1, model_width),
        slot_grad.reshape(-1, model_width),
        gate_mat,
        up_mat,
        down_mat,
    )
    slot_scores = jnp.einsum(
        "ncd,ncd->nc", grad_rows, back_out.reshape(block_shape), preferred_element_type=jnp.float32
    ).astype(jnp.bfloat16)
    returned_f = lax.all_to_all(
        front_out.reshape(block_shape), "expert", split_axis=0, concat_axis=0, tiled=True
    )
    returned_dn = lax.all_to_all(
        back_grad.reshape(block_shape), "expert", split_axis=0, concat_axis=0, tiled=True
    )
    returned_s = lax.all_to_all(slot_scores, "expert", split_axis=0, concat_axis=0, tiled=True)
    scores_b = jnp.take(returned_s.reshape(slot_count), position_b, axis=0)
    scores = lax.optimization_barrier(scores_b).astype(jnp.float32)
    picked_f = jnp.take(returned_f.reshape(slot_count, model_width), position_f, axis=0)
    combined = jnp.sum(weights_f[:, :, None] * picked_f.astype(jnp.float32), axis=1)
    layer_out = (arrived.astype(jnp.float32) + combined).astype(jnp.bfloat16)
    picked_dn = jnp.take(returned_dn.reshape(slot_count, model_width), position_b, axis=0)
    grad_normed = jnp.sum(picked_dn.astype(jnp.float32), axis=1)
    grad_normed = grad_normed + router_backward(
        scores, weights_b, sig_b, tot_b, match_b, router_mat
    )
    input_grad = cotangent.astype(jnp.float32) + norm_backward(
        stored, inverse_b, gain_row, grad_normed
    )
    return (layer_out[None], input_grad.astype(jnp.bfloat16)[None])


def solution(mesh):
    placed = (
        P("section", "expert", None),
        P("section", "expert", None),
        P("section", "expert", None),
        P("section", None),
        P("section", None, None),
        P("section", "expert", None, None),
        P("section", "expert", None, None),
        P("section", "expert", None, None),
        P("section", "expert", None),
        P("section", "expert", None),
    )
    return jax.shard_map(
        body,
        mesh=mesh,
        in_specs=placed,
        out_specs=(P("section", "expert", None), P("section", "expert", None)),
        check_vma=False,
    )
```

profile of v0, /device:TPU:0, one launch (start us, length us, event | category | flops | bytes accessed | tf_op | source)
XLA Modules:
  0.0 174.8 jit_solution(11579886633371574897)
XLA Ops:
  0.7 5.1 %collective-permute-start.1 = (bf16[1,128,2048]{2,1,0:T(8,128)(2,1)}, bf16[1,128,2048]{2,1,0:T(8,128)(2,1)}, u32[]{:S(2)}, u32[]{:S(2)}) collective-permute-start(bf16[1,128,2048]{2,1,0:T(8,128)(2,1)} %param.13), channel_id=1, source_target_pairs={{0,24},{8,0},{16,8},{24,16},{1,25},{9,1},{17,9},{25,17},{2,26},{10... | collective-permute-start | bytes 1572872 | tf_op jit(solution)/shard_map/ppermute | solution.py:12
  11.8 3.7 %all-to-all-start.2 = ((bf16[8,1,48]{2,1,0:T(2,128)(2,1)}), bf16[8,1,48]{2,1,0:T(2,128)(2,1)S(1)}, u32[]{:S(2)}, u32[]{:S(2)}) async-start(bf16[8,1,48]{2,1,0:T(2,128)(2,1)} %all_to_all.36), calls=%async_computation.2 | async-start | bytes 8192 | tf_op jit(solution)/shard_map/all_to_all | solution.py:135
  15.6 2.9 %convolution_convert_fusion = bf16[384,2048]{1,0:T(8,128)(2,1)} fusion(bf16[1,128,2048]{2,1,0:T(8,128)(2,1)} %param.14, f32[128]{0:T(128)S(1)} %get-tuple-element.17, f32[2048]{0:T(1024)S(1)} %bitcast.157, bf16[384,128]{1,0:T(8,128)(2,1)S(1)} %get-tuple-element.4), kind=kOutput, calls=%fused_computation.28 | convolution fusion | flops 203161600 | bytes 2204160 | tf_op jit(solution)/shard_map/dot_general | solution.py:119
  20.1 4.4 %all-to-all-start.4 = ((bf16[8,48,2048]{2,1,0:T(8,128)(2,1)}), bf16[8,48,2048]{2,1,0:T(8,128)(2,1)}, u32[]{:S(2)}, u32[]{:S(2)}) async-start(bf16[8,48,2048]{2,1,0:T(8,128)(2,1)} %bitcast.149), calls=%async_computation.4 | async-start | bytes 3145728 | tf_op jit(solution)/shard_map/all_to_all | solution.py:133
  25.0 6.9 %collective-permute-done = bf16[1,128,2048]{2,1,0:T(8,128)(2,1)} collective-permute-done((bf16[1,128,2048]{2,1,0:T(8,128)(2,1)}, bf16[1,128,2048]{2,1,0:T(8,128)(2,1)}, u32[]{:S(2)}, u32[]{:S(2)}) %collective-permute-start) | collective-permute-done | bytes 524320 | tf_op jit(solution)/shard_map/ppermute | solution.py:12
  34.6 2.7 %convolution_convert_fusion.1 = bf16[384,2048]{1,0:T(8,128)(2,1)} fusion(bf16[1,128,2048]{2,1,0:T(8,128)(2,1)} %collective-permute-done.1, bf16[384,128]{1,0:T(8,128)(2,1)S(1)} %get-tuple-element.4), kind=kOutput, calls=%fused_computation.29 | convolution fusion | flops 202113024 | bytes 2195456 | tf_op jit(solution)/shard_map/dot_general | solution.py:123
  37.4 8.2 %all-to-all-done.4 = bf16[8,48,2048]{2,1,0:T(8,128)(2,1)} async-done(((bf16[8,48,2048]{2,1,0:T(8,128)(2,1)}), bf16[8,48,2048]{2,1,0:T(8,128)(2,1)}, u32[]{:S(2)}, u32[]{:S(2)}) %all-to-all-start.4) | async-done | bytes 1572896 | tf_op jit(solution)/shard_map/all_to_all | solution.py:133
  45.6 4.3 %all-to-all-start.3 = ((bf16[8,48,2048]{2,1,0:T(8,128)(2,1)}), bf16[8,48,2048]{2,1,0:T(8,128)(2,1)}, u32[]{:S(2)}, u32[]{:S(2)}) async-start(bf16[8,48,2048]{2,1,0:T(8,128)(2,1)} %bitcast.151), calls=%async_computation.3 | async-start | bytes 3145728 | tf_op jit(solution)/shard_map/all_to_all | solution.py:134
  50.0 2.9 %convolution_convert_fusion.2 = bf16[384,2048]{1,0:T(8,128)(2,1)} fusion(bf16[1,128,2048]{2,1,0:T(8,128)(2,1)} %collective-permute-done, f32[2048]{0:T(1024)S(1)} %bitcast.159, f32[128]{0:T(128)S(1)} %add_rsqrt_fusion.1, bf16[384,128]{1,0:T(8,128)(2,1)S(1)} %select_reduce_fusion.2), kind=kOutput, calls=%fused_computation.30 | convolution fusion | flops 203161600 | bytes 2204160 | tf_op jit(solution)/shard_map/dot_general | solution.py:113
  52.9 5.0 %fusion.16 = f32[384,768]{1,0:T(8,128)} fusion(bf16[384,2048]{1,0:T(8,128)(2,1)} %bitcast.25, bf16[1,1,2048,768]{3,2,1,0:T(8,128)(2,1)} %param.17), kind=kOutput, calls=%fused_computation.21 | convolution fusion | flops 1207959552 | bytes 5898240 | tf_op jit(solution)/shard_map/dot_general | solution.py:48
  57.8 3.8 %fusion.10 = f32[384,768]{1,0:T(8,128)} fusion(bf16[384,2048]{1,0:T(8,128)(2,1)} %bitcast.25, bf16[1,1,2048,768]{3,2,1,0:T(8,128)(2,1)S(1)} %copy-done.7), kind=kOutput, calls=%fused_computation.15 | convolution fusion | flops 1207959552 | bytes 5898240 | tf_op jit(solution)/shard_map/dot_general | solution.py:49
  61.7 9.2 %all-to-all-done.3 = bf16[8,48,2048]{2,1,0:T(8,128)(2,1)} async-done(((bf16[8,48,2048]{2,1,0:T(8,128)(2,1)}), bf16[8,48,2048]{2,1,0:T(8,128)(2,1)}, u32[]{:S(2)}, u32[]{:S(2)}) %all-to-all-start.3) | async-done | bytes 1572896 | tf_op jit(solution)/shard_map/all_to_all | solution.py:134
  70.9 4.3 %all-to-all-start = ((bf16[8,48,2048]{2,1,0:T(8,128)(2,1)}), bf16[8,48,2048]{2,1,0:T(8,128)(2,1)}, u32[]{:S(2)}, u32[]{:S(2)}) async-start(bf16[8,48,2048]{2,1,0:T(8,128)(2,1)} %bitcast.150), calls=%async_computation | async-start | bytes 3145728 | tf_op jit(solution)/shard_map/all_to_all | solution.py:132
  75.2 3.0 %fusion.25 = bf16[384,2048]{1,0:T(8,128)(2,1)S(1)} fusion(bf16[1,1,768,2048]{3,2,1,0:T(8,128)(2,1)S(1)} %copy-done, f32[384,768]{1,0:T(8,128)} %fusion.10, f32[384,768]{1,0:T(8,128)} %fusion.16), kind=kOutput, calls=%fused_computation.27 | convolution fusion | flops 1210515456 | bytes 7077888 | tf_op jit(solution)/shard_map/dot_general | solution.py:51
  78.3 2.1 %fusion.1 = (bf16[8,48]{1,0:T(8,128)(2,1)S(1)}, bf16[8,48,2048]{2,1,0:T(8,128)(2,1)S(1)}) fusion(bf16[8,48,2048]{2,1,0:T(8,128)(2,1)} %all-to-all-done.3, bf16[8,48,2048]{2,1,0:T(8,128)(2,1)S(1)} %bitcast.153, f32[8,48]{1,0:T(8,128)S(1)} %bitcast.168), kind=kLoop, calls=%fused_computation.6 | loop fusion | flops 4718208 | bytes 4720896 | tf_op jit(solution)/shard_map/ncd,ncd->nc/dot_general | solution.py:148
  83.6 3.1 %fusion.8 = f32[384,2048]{1,0:T(8,128)} fusion(bf16[1,1,2048,768]{3,2,1,0:T(8,128)(2,1)S(1)} %copy-done.8, f32[384,768]{1,0:T(8,128)S(1)} %fusion.4, f32[384,768]{1,0:T(8,128)S(1)} %copy-done.9), kind=kOutput, calls=%fused_computation.13 | convolution fusion | flops 1209729024 | bytes 8650752 | tf_op jit(solution)/shard_map/dot_general | solution.py:65
  86.7 9.5 %all-to-all-done = bf16[8,48,2048]{2,1,0:T(8,128)(2,1)} async-done(((bf16[8,48,2048]{2,1,0:T(8,128)(2,1)}), bf16[8,48,2048]{2,1,0:T(8,128)(2,1)}, u32[]{:S(2)}, u32[]{:S(2)}) %all-to-all-start) | async-done | bytes 1572896 | tf_op jit(solution)/shard_map/all_to_all | solution.py:132
  96.3 3.5 %all-to-all-start.6 = ((bf16[8,1,48]{2,1,0:T(2,128)(2,1)}), bf16[8,1,48]{2,1,0:T(2,128)(2,1)S(1)}, u32[]{:S(2)}, u32[]{:S(2)}) async-start(bf16[8,1,48]{2,1,0:T(2,128)(2,1)} %copy.58), calls=%async_computation.6 | async-start | bytes 8192 | tf_op jit(solution)/shard_map/all_to_all | solution.py:157
  99.8 6.8 %add_convert_fusion = bf16[384,2048]{1,0:T(8,128)(2,1)} fusion(f32[384,2048]{1,0:T(8,128)} %fusion.8, bf16[1,1,2048,768]{3,2,1,0:T(8,128)(2,1)} %param.17, f32[384,768]{1,0:T(8,128)} %fusion.16, f32[384,768]{1,0:T(8,128)} %copy-done.10, f32[384,768]{1,0:T(8,128)} %fusion.10), kind=kOutput, calls=%fused_computation.25 | convolution fusion | flops 1212481536 | bytes 11403264 | tf_op jit(solution)/shard_map/dot_general | solution.py:64
  106.5 4.3 %all-to-all-start.5 = ((bf16[8,48,2048]{2,1,0:T(8,128)(2,1)}), bf16[8,48,2048]{2,1,0:T(8,128)(2,1)}, u32[]{:S(2)}, u32[]{:S(2)}) async-start(bf16[8,48,2048]{2,1,0:T(8,128)(2,1)} %bitcast.155), calls=%async_computation.5 | async-start | bytes 3145728 | tf_op jit(solution)/shard_map/all_to_all | solution.py:154
  110.8 4.8 %fusion.18 = f32[384,768]{1,0:T(8,128)} fusion(bf16[384,2048]{1,0:T(8,128)(2,1)} %bitcast.8, bf16[1,1,2048,768]{3,2,1,0:T(8,128)(2,1)} %param.17), kind=kOutput, calls=%fused_computation.23 | convolution fusion | flops 1207959552 | bytes 5898240 | tf_op jit(solution)/shard_map/dot_general | solution.py:48
  115.6 6.9 %fusion.22 = bf16[384,2048]{1,0:T(8,128)(2,1)} fusion(bf16[1,1,768,2048]{3,2,1,0:T(8,128)(2,1)S(1)} %copy-done, bf16[384,2048]{1,0:T(8,128)(2,1)} %bitcast.8, bf16[1,1,2048,768]{3,2,1,0:T(8,128)(2,1)} %param.18, f32[384,768]{1,0:T(8,128)} %fusion.18), kind=kOutput, calls=%fused_computation.26 | convolution fusion | flops 2418475008 | bytes 10616832 | tf_op jit(solution)/shard_map/dot_general | solution.py:51
  125.2 6.7 %all-to-all-done.5 = bf16[8,48,2048]{2,1,0:T(8,128)(2,1)} async-done(((bf16[8,48,2048]{2,1,0:T(8,128)(2,1)}), bf16[8,48,2048]{2,1,0:T(8,128)(2,1)}, u32[]{:S(2)}, u32[]{:S(2)}) %all-to-all-start.5) | async-done | bytes 1572896 | tf_op jit(solution)/shard_map/all_to_all | solution.py:154
  131.9 4.3 %all-to-all-start.1 = ((bf16[8,48,2048]{2,1,0:T(8,128)(2,1)}), bf16[8,48,2048]{2,1,0:T(8,128)(2,1)}, u32[]{:S(2)}, u32[]{:S(2)}) async-start(bf16[8,48,2048]{2,1,0:T(8,128)(2,1)} %bitcast.154), calls=%async_computation.1 | async-start | bytes 3145728 | tf_op jit(solution)/shard_map/all_to_all | solution.py:151
  136.2 5.0 %gather_fusion.2 = bf16[256,2048]{1,0:T(8,128)(2,1)} fusion(bf16[384,2048]{1,0:T(8,128)(2,1)} %bitcast.27, s32[1024]{0:T(1024)S(1)} %pad_clamp_fusion.1), kind=kCustom, calls=%fused_computation.1.clone | custom fusion | bytes 2098176 | tf_op jit(solution)/shard_map/jit(_take)/gather | solution.py:163
  141.2 2.5 %reshape.256 = bf16[128,2,2048]{2,1,0:T(2,128)(2,1)} reshape(bf16[256,2048]{1,0:T(8,128)(2,1)} %gather_fusion.2) | data formatting | bytes 2097152 | tf_op jit(solution)/shard_map/jit(_take)/gather | solution.py:163
  143.7 5.2 %convert_reduce_fusion = f32[128,2048]{1,0:T(8,128)S(1)} fusion(bf16[128,2,2048]{2,1,0:T(2,128)(2,1)} %reshape.256, pred[128,2]{1,0:T(8,128)(4,1)S(1)} %copy.55), kind=kLoop, calls=%fused_computation.33 | loop fusion | flops 1310720 | bytes 2097408 | tf_op jit(solution)/shard_map/reduce_sum | solution.py:164
  150.7 6.5 %all-to-all-done.1 = bf16[8,48,2048]{2,1,0:T(8,128)(2,1)} async-done(((bf16[8,48,2048]{2,1,0:T(8,128)(2,1)}), bf16[8,48,2048]{2,1,0:T(8,128)(2,1)}, u32[]{:S(2)}, u32[]{:S(2)}) %all-to-all-start.1) | async-done | bytes 1572896 | tf_op jit(solution)/shard_map/all_to_all | solution.py:151
  157.2 5.0 %gather_fusion.1 = bf16[256,2048]{1,0:T(8,128)(2,1)} fusion(bf16[384,2048]{1,0:T(8,128)(2,1)} %bitcast.13, s32[1024]{0:T(1024)S(1)} %pad_clamp_fusion.2), kind=kCustom, calls=%fused_computation.clone | custom fusion | bytes 2098176 | tf_op jit(solution)/shard_map/jit(_take)/gather | solution.py:160
  162.2 2.5 %reshape.252 = bf16[128,2,2048]{2,1,0:T(2,128)(2,1)} reshape(bf16[256,2048]{1,0:T(8,128)(2,1)} %gather_fusion.1) | data formatting | bytes 2097152 | tf_op jit(solution)/shard_map/jit(_take)/gather | solution.py:160
  164.7 5.7 %multiply_reduce_fusion = f32[128,2048]{1,0:T(8,128)S(1)} fusion(bf16[128,2,2048]{2,1,0:T(2,128)(2,1)} %reshape.252, pred[128,2]{1,0:T(8,128)(4,1)S(1)} %copy.50, f32[128,2]{1,0:T(8,128)S(1)} %copy.46), kind=kLoop, calls=%fused_computation.34 | loop fusion | flops 1835008 | bytes 2098432 | tf_op jit(solution)/shard_map/reduce_sum | solution.py:161
  172.5 2.3 %fusion.70 = bf16[1,128,2048]{2,1,0:T(8,128)(2,1)} fusion(bf16[1,128,2048]{2,1,0:T(8,128)(2,1)S(1)} %copy-done.2, f32[128,2048]{1,0:T(8,128)S(1)} %copy-done.3, bf16[1,128,2048]{2,1,0:T(8,128)(2,1)} %collective-permute-done.1, f32[128]{0:T(128)S(1)} %broadcast_multiply_fusion, f32[128]{0:T(128)S(1)} %get-tuple-element.16, f32[128]{0:T(128)S(1)} %get-tuple-element.17), kind=kLoop, calls=%fused_computation.78 | loop fusion | flops 2097152 | bytes 2622976 | tf_op jit(solution)/shard_map/broadcast_in_dim | solution.py:171
  (87 shorter events, 20.7 us)
Async XLA Ops:
  0.6 74.6 %copy-start = (bf16[1,1,768,2048]{3,2,1,0:T(8,128)(2,1)S(1)}, bf16[1,1,768,2048]{3,2,1,0:T(8,128)(2,1)}, u32[]{:S(2)}) copy-start(bf16[1,1,768,2048]{3,2,1,0:T(8,128)(2,1)} %param.19) | copy-start | bytes 9437188
  0.6 10.2 %copy-start.4 = (s32[1,128,2]{1,2,0:T(2,128)S(1)}, s32[1,128,2]{1,2,0:T(2,128)}, u32[]{:S(2)}) copy-start(s32[1,128,2]{1,2,0:T(2,128)} %param.21) | copy-start | bytes 3076
  0.7 34.0 %collective-permute-start.1 = (bf16[1,128,2048]{2,1,0:T(8,128)(2,1)}, bf16[1,128,2048]{2,1,0:T(8,128)(2,1)}, u32[]{:S(2)}, u32[]{:S(2)}) collective-permute-start(bf16[1,128,2048]{2,1,0:T(8,128)(2,1)} %param.13), channel_id=1, source_target_pairs={{0,24},{8,0},{16,8},{24,16},{1,25},{9,1},{17,9},{25,17},{2,26},{10... | collective-permute-start | bytes 1572872 | tf_op jit(solution)/shard_map/ppermute | solution.py:12
  9.8 8.7 %copy-start.6 = (s32[1,128,2]{1,2,0:T(2,128)S(1)}, s32[1,128,2]{1,2,0:T(2,128)}, u32[]{:S(2)}) copy-start(s32[1,128,2]{1,2,0:T(2,128)} %param.20) | copy-start | bytes 3076
  11.8 8.3 %all-to-all-start.2 = ((bf16[8,1,48]{2,1,0:T(2,128)(2,1)}), bf16[8,1,48]{2,1,0:T(2,128)(2,1)S(1)}, u32[]{:S(2)}, u32[]{:S(2)}) async-start(bf16[8,1,48]{2,1,0:T(2,128)(2,1)} %all_to_all.36), calls=%async_computation.2 | async-start | bytes 8192 | tf_op jit(solution)/shard_map/all_to_all | solution.py:135
  15.5 16.4 %collective-permute-start = (bf16[1,128,2048]{2,1,0:T(8,128)(2,1)}, bf16[1,128,2048]{2,1,0:T(8,128)(2,1)}, u32[]{:S(2)}, u32[]{:S(2)}) collective-permute-start(bf16[1,128,2048]{2,1,0:T(8,128)(2,1)} %param.12), channel_id=1, source_target_pairs={{0,8},{8,16},{16,24},{24,0},{1,9},{9,17},{17,25},{25,1},{2,10},{10... | collective-permute-start | bytes 1572872 | tf_op jit(solution)/shard_map/ppermute | solution.py:12
  20.1 13.1 %copy-start.5 = (bf16[1,2048,8]{1,2,0:T(8,128)(2,1)S(1)}, bf16[1,2048,8]{1,2,0:T(8,128)(2,1)}, u32[]{:S(2)}) copy-start(bf16[1,2048,8]{1,2,0:T(8,128)(2,1)} %param.16) | copy-start | bytes 98308
  20.1 25.5 %all-to-all-start.4 = ((bf16[8,48,2048]{2,1,0:T(8,128)(2,1)}), bf16[8,48,2048]{2,1,0:T(8,128)(2,1)}, u32[]{:S(2)}, u32[]{:S(2)}) async-start(bf16[8,48,2048]{2,1,0:T(8,128)(2,1)} %bitcast.149), calls=%async_computation.4 | async-start | bytes 3145728 | tf_op jit(solution)/shard_map/all_to_all | solution.py:133
  45.6 25.3 %all-to-all-start.3 = ((bf16[8,48,2048]{2,1,0:T(8,128)(2,1)}), bf16[8,48,2048]{2,1,0:T(8,128)(2,1)}, u32[]{:S(2)}, u32[]{:S(2)}) async-start(bf16[8,48,2048]{2,1,0:T(8,128)(2,1)} %bitcast.151), calls=%async_computation.3 | async-start | bytes 3145728 | tf_op jit(solution)/shard_map/all_to_all | solution.py:134
  52.9 5.0 %copy-start.7 = (bf16[1,1,2048,768]{3,2,1,0:T(8,128)(2,1)S(1)}, bf16[1,1,2048,768]{3,2,1,0:T(8,128)(2,1)}, u32[]{:S(2)}) copy-start(bf16[1,1,2048,768]{3,2,1,0:T(8,128)(2,1)} %param.18) | copy-start | bytes 9437188
  70.9 25.3 %all-to-all-start = ((bf16[8,48,2048]{2,1,0:T(8,128)(2,1)}), bf16[8,48,2048]{2,1,0:T(8,128)(2,1)}, u32[]{:S(2)}, u32[]{:S(2)}) async-start(bf16[8,48,2048]{2,1,0:T(8,128)(2,1)} %bitcast.150), calls=%async_computation | async-start | bytes 3145728 | tf_op jit(solution)/shard_map/all_to_all | solution.py:132
  81.0 2.6 %copy-start.8 = (bf16[1,1,2048,768]{3,2,1,0:T(8,128)(2,1)S(1)}, bf16[1,1,2048,768]{3,2,1,0:T(8,128)(2,1)}, u32[]{:S(2)}) copy-start(bf16[1,1,2048,768]{3,2,1,0:T(8,128)(2,1)} %param.18) | copy-start | bytes 9437188
  81.0 2.6 %copy-start.9 = (f32[384,768]{1,0:T(8,128)S(1)}, f32[384,768]{1,0:T(8,128)}, u32[]{:S(2)}) copy-start(f32[384,768]{1,0:T(8,128)} %fusion.16) | copy-start | bytes 3538948
  82.5 1.1 copy-start.10
  96.3 10.3 %all-to-all-start.6 = ((bf16[8,1,48]{2,1,0:T(2,128)(2,1)}), bf16[8,1,48]{2,1,0:T(2,128)(2,1)S(1)}, u32[]{:S(2)}, u32[]{:S(2)}) async-start(bf16[8,1,48]{2,1,0:T(2,128)(2,1)} %copy.58), calls=%async_computation.6 | async-start | bytes 8192 | tf_op jit(solution)/shard_map/all_to_all | solution.py:157
  106.5 25.3 %all-to-all-start.5 = ((bf16[8,48,2048]{2,1,0:T(8,128)(2,1)}), bf16[8,48,2048]{2,1,0:T(8,128)(2,1)}, u32[]{:S(2)}, u32[]{:S(2)}) async-start(bf16[8,48,2048]{2,1,0:T(8,128)(2,1)} %bitcast.155), calls=%async_computation.5 | async-start | bytes 3145728 | tf_op jit(solution)/shard_map/all_to_all | solution.py:154
  131.9 25.3 %all-to-all-start.1 = ((bf16[8,48,2048]{2,1,0:T(8,128)(2,1)}), bf16[8,48,2048]{2,1,0:T(8,128)(2,1)}, u32[]{:S(2)}, u32[]{:S(2)}) async-start(bf16[8,48,2048]{2,1,0:T(8,128)(2,1)} %bitcast.154), calls=%async_computation.1 | async-start | bytes 3145728 | tf_op jit(solution)/shard_map/all_to_all | solution.py:151
  143.7 5.2 %copy-start.1 = (bf16[1,128,2048]{2,1,0:T(8,128)(2,1)S(1)}, bf16[1,128,2048]{2,1,0:T(8,128)(2,1)}, u32[]{:S(2)}) copy-start(bf16[1,128,2048]{2,1,0:T(8,128)(2,1)} %param.14) | copy-start | bytes 1572868
  170.4 2.1 %copy-start.2 = (bf16[1,128,2048]{2,1,0:T(8,128)(2,1)S(1)}, bf16[1,128,2048]{2,1,0:T(8,128)(2,1)}, u32[]{:S(2)}) copy-start(bf16[1,128,2048]{2,1,0:T(8,128)(2,1)} %param.14) | copy-start | bytes 1572868
  170.4 2.1 %copy-start.3 = (f32[128,2048]{1,0:T(8,128)S(1)}, f32[128,2048]{1,0:T(8,128)}, u32[]{:S(2)}) copy-start(f32[128,2048]{1,0:T(8,128)} %get-tuple-element.19) | copy-start | bytes 3145732
where the time goes:
time: 176 us; the launch traced here: 175 us
  waiting for transfers between devices  48.1 us (27%)
  matrix products  47.8 us (27%)
  starting transfers between devices  33.9 us (19%)
  other arithmetic  22.9 us (13%)
  local copies, waits for them, and re-layouts  21.1 us (12%)
    dot_general x2, matrix products, expert_forward(): jnp.dot(hidden, down_mat, preferred_element_type=jnp.float32)  9.93 us
    dot_general x2, matrix products, expert_forward(): gate = jnp.dot(slot_rows, gate_mat, preferred_element_type=jnp.float32)  9.71 us
    all_to_all x1, waiting for transfers between devices, body(): lax.all_to_all(buffer_f, 'expert', split_axis=0, concat_axis=0, tiled=True)  9.53 us
    all_to_all x1, waiting for transfers between devices, body(): lax.all_to_all(grad_buffer, 'expert', split_axis=0, concat_axis=0, tiled=...  9.22 us
    all_to_all x1, waiting for transfers between devices, body(): lax.all_to_all(buffer_b, 'expert', split_axis=0, concat_axis=0, tiled=True)  8.2 us
    gather x2, local copies, waits for them, and re-layouts, body(): jnp.take(returned_f.reshape(slot_count, model_width), position_f, axis=0)  7.51 us
    gather x2, local copies, waits for them, and re-layouts, body(): jnp.take(returned_dn.reshape(slot_count, model_width), position_b, axis=0)  7.5 us
    ppermute x2, waiting for transfers between devices, passed_along(): return lax.ppermute(value, axis, pairs)  6.95 us
  transfers between devices with their start and end apart: 9, of which 7 were waited for; matrix products, arithmetic and copies ran while one was open for 41% of the time, Pallas kernels for 0%

commit v1 on v0

v1 whole, which is shorter than its diff:
```python
import functools

import jax
import jax.numpy as jnp
from jax import lax
from jax.experimental import pallas as pl
from jax.experimental.pallas import tpu as pltpu
from jax.sharding import PartitionSpec as P

NORM_EPS = 1e-06
LANES = 128
CHUNK = 256
F32, BF16 = jnp.float32, jnp.bfloat16
MESH = pl.DeviceIdType.MESH
NN = (((1,), (0,)), ((), ()))
NT = (((1,), (1,)), ((), ()))
ROW_B, ROW_C, ROW_F, OUT_G, OUT_F = range(5)


def mm(left, right, dims=NN):
    return lax.dot_general(left, right, dims, preferred_element_type=F32)


def halves(value):
    high = value.astype(BF16)
    return high, (value - high.astype(F32)).astype(BF16)


def chunks(width, step, work):
    @pl.loop(0, width // step)
    def _(index):
        work(pl.ds(pl.multiple_of(index * step, step), step))


def inverse_rms(values):
    return lax.rsqrt(jnp.mean(values * values, axis=1, keepdims=True) + NORM_EPS)


def places(routes, top, capacity):
    rows = routes.shape[0]
    columns = lax.broadcasted_iota(jnp.int32, (rows, LANES), 1)
    matches = [(routes[:, k : k + 1] == columns).astype(F32) for k in range(top)]
    per_row = sum(matches)
    before = lax.broadcasted_iota(jnp.int32, (rows, rows), 1) < lax.broadcasted_iota(
        jnp.int32, (rows, rows), 0
    )
    earlier = mm(before.astype(F32).astype(BF16), per_row.astype(BF16))
    offsets = earlier + columns.astype(F32) * capacity
    return matches, [jnp.sum(m * offsets, axis=1, keepdims=True) for m in matches]


def route_weights(normed, router, matches):
    logits = mm(normed, router)
    sig = [jax.nn.sigmoid(jnp.sum(m * logits, axis=1, keepdims=True)) for m in matches]
    total = sum(sig)
    return [s / total for s in sig], sig, total


def table(positions, scales, slots):
    rows = positions[0].shape[0]
    columns = lax.broadcasted_iota(jnp.int32, (rows, slots), 1).astype(F32)
    return sum(jnp.where(columns == p, s, 0.0) for p, s in zip(positions, scales))


def kernel(
    owners, sections, capacity, top,
    act_ref, grad_ref, stored_ref, gain_ref, router_ref, routes_f_ref, routes_b_ref,
    gate_hbm, up_hbm, down_hbm,
    layer_ref, input_ref,
    gate_w, up_w, down_w, arrived, cot,
    send_b, send_c, send_f, send_g, send_o,
    recv_b, recv_c, recv_f, recv_g, recv_o,
    normed, gate, upper, hidden, slot_grad, out_b, grad_gate, grad_up, acc,
    weight_sem, hop_send, hop_recv, send_sem, recv_sem,
):
    slots = owners * capacity
    width = act_ref.shape[1]
    hidden_width = gate_w.shape[1]
    me = lax.axis_index("expert")
    section = lax.axis_index("section")
    after = lax.rem(section + 1, sections)
    before = lax.rem(section + sections - 1, sections)
    sends = (send_b, send_c, send_f, send_g, send_o)
    recvs = (recv_b, recv_c, recv_f, recv_g, recv_o)

    loads = [
        pltpu.make_async_copy(source, target, weight_sem.at[i])
        for i, (source, target) in enumerate(
            ((gate_hbm, gate_w), (up_hbm, up_w), (down_hbm, down_w))
        )
    ]
    for load in loads:
        load.start()

    barrier = pltpu.get_barrier_semaphore()

    @pl.loop(1, owners)
    def _(step):
        pl.semaphore_signal(
            barrier, inc=1, device_id={"expert": lax.rem(me + step, owners)}, device_id_type=MESH
        )

    for neighbour in (after, before):
        pl.semaphore_signal(barrier, inc=1, device_id={"section": neighbour}, device_id_type=MESH)
    pl.semaphore_wait(barrier, owners + 1)

    def rows_of(index):
        return pl.ds(pl.multiple_of(index * capacity, 16), capacity)

    def block_copy(kind, step):
        peer = lax.rem(me + step, owners)
        return pltpu.make_async_remote_copy(
            src_ref=sends[kind].at[rows_of(peer)],
            dst_ref=recvs[kind].at[rows_of(me)],
            send_sem=send_sem.at[kind, step],
            recv_sem=recv_sem.at[kind, step],
            device_id={"expert": peer},
            device_id_type=MESH,
        )

    def send(kind):
        @pl.loop(1, owners)
        def _(step):
            block_copy(kind, step).start()

        recvs[kind][rows_of(me)] = sends[kind][rows_of(me)]

    def receive(kind):
        @pl.loop(1, owners)
        def _(step):
            source = lax.rem(me + owners - step, owners)
            pltpu.make_async_remote_copy(
                src_ref=sends[kind].at[rows_of(source)],
                dst_ref=recvs[kind].at[rows_of(source)],
                send_sem=send_sem.at[kind, step],
                recv_sem=recv_sem.at[kind, step],
                device_id={"expert": source},
                device_id_type=MESH,
            ).wait_recv()

    def hop(index, source, target, neighbour):
        return pltpu.make_async_remote_copy(
            src_ref=source, dst_ref=target,
            send_sem=hop_send.at[index], recv_sem=hop_recv.at[index],
            device_id={"section": neighbour}, device_id_type=MESH,
        )

    grad_hop = hop(0, grad_ref, cot, before)
    act_hop = hop(1, act_ref, arrived, after)
    grad_hop.start()

    gain = gain_ref[...].astype(F32)
    router = router_ref[...]
    ones = [1.0] * top

    match_b, pos_b = places(routes_b_ref[...], top, capacity)
    values = stored_ref[...].astype(F32)
    inverse_b = inverse_rms(values)
    normed[...] = (values * inverse_b * gain).astype(BF16)
    spread_b = table(pos_b, ones, slots).T.astype(BF16)

    def fill_b(cols):
        send_b[:, cols] = mm(spread_b, normed[:, cols]).astype(BF16)

    chunks(width, CHUNK, fill_b)
    send(ROW_B)
    weights_b, sig_b, total_b = route_weights(normed[...], router, match_b)
    scales = [w.astype(BF16).astype(F32) for w in weights_b]
    scale_table = table(pos_b, scales, slots).T.astype(BF16)
    send_c[:, width:] = mm(scale_table, jnp.ones((scale_table.shape[1], LANES), BF16)).astype(BF16)

    grad_hop.wait()
    act_hop.start()

    def fill_c(cols):
        send_c[:, cols] = mm(spread_b, cot[:, cols]).astype(BF16)

    chunks(width, CHUNK, fill_c)
    send(ROW_C)

    def expert_hidden(rows_ref, keep):
        def work(cols):
            g = mm(rows_ref[...], gate_w[:, cols])
            u = mm(rows_ref[...], up_w[:, cols])
            if keep:
                gate[:, cols] = g
                upper[:, cols] = u
            hidden[:, cols] = (g * jax.nn.sigmoid(g) * u).astype(BF16)

        chunks(hidden_width, CHUNK, work)

    def expert_down(target):
        def work(cols):
            target[:, cols] = mm(hidden[...], down_w[:, cols]).astype(BF16)

        chunks(width, CHUNK, work)

    for load in loads:
        load.wait()
    receive(ROW_B)
    expert_hidden(recv_b, True)

    match_f, pos_f = places(routes_f_ref[...], top, capacity)
    spread_f = table(pos_f, ones, slots).T.astype(BF16)
    act_hop.wait()
    values = arrived[...].astype(F32)
    normed[...] = (values * inverse_rms(values) * gain).astype(BF16)

    def fill_f(cols):
        send_f[:, cols] = mm(spread_f, normed[:, cols]).astype(BF16)

    chunks(width, CHUNK, fill_f)
    send(ROW_F)
    weights_f = route_weights(normed[...], router, match_f)[0]
    expert_down(out_b)

    receive(ROW_C)
    acc[...] = jnp.zeros_like(acc)
    scale = recv_c[:, width:].astype(F32)[:, :1]

    def scale_rows(cols):
        rows = recv_c[:, cols].astype(F32)
        slot_grad[:, cols] = (scale * rows).astype(BF16)
        product = rows * out_b[:, cols].astype(F32)
        acc[...] += product[:, :LANES] + product[:, LANES:]

    chunks(width, CHUNK, scale_rows)

    def hidden_grads(cols):
        grad_hidden = mm(slot_grad[...], down_w[cols, :], NT)
        g = gate[:, cols]
        s = jax.nn.sigmoid(g)
        grad_up[:, cols] = (grad_hidden * g * s).astype(BF16)
        grad_gate[:, cols] = (
            grad_hidden * upper[:, cols] * s * (1.0 + g * (1.0 - s))
        ).astype(BF16)

    chunks(hidden_width, CHUNK, hidden_grads)

    def row_grads(cols):
        total = mm(grad_gate[...], gate_w[cols, :], NT) + mm(grad_up[...], up_w[cols, :], NT)
        send_g[:, cols] = total.astype(BF16)

    chunks(width, CHUNK, row_grads)
    scores = jnp.sum(acc[...], axis=1, keepdims=True)
    send_g[:, width:] = jnp.broadcast_to(scores, (slots, LANES)).astype(BF16)
    send(OUT_G)

    receive(ROW_F)
    expert_hidden(recv_f, False)
    expert_down(send_o)
    send(OUT_F)

    receive(OUT_G)
    score = [
        mm(table([p], [1.0], slots).astype(BF16), recv_g[:, width:])[:, :1] for p in pos_b
    ]
    mixed = sum(w * s for w, s in zip(weights_b, score))
    grad_logits = sum(
        (s - mixed) / total_b * g * (1.0 - g) * m for s, g, m in zip(score, sig_b, match_b)
    )
    logits_high, logits_low = halves(grad_logits)
    gather_b = table(pos_b, ones, slots).astype(BF16)
    grad_normed = (
        mm(gather_b, recv_g[:, :width])
        + mm(logits_high, router, NT)
        + mm(logits_low, router, NT)
    )
    grad_pre = grad_normed * gain
    values = stored_ref[...].astype(F32)
    mean = jnp.mean(grad_pre * values, axis=1, keepdims=True)
    input_ref[...] = (
        cot[...].astype(F32)
        + inverse_b * grad_pre
        - values * (inverse_b * inverse_b * inverse_b) * mean
    ).astype(BF16)

    weight_high, weight_low = halves(table(pos_f, weights_f, slots))
    receive(OUT_F)

    def combine(cols):
        rows = recv_o[:, cols]
        mixed_rows = mm(weight_high, rows) + mm(weight_low, rows)
        layer_ref[:, cols] = (arrived[:, cols].astype(F32) + mixed_rows).astype(BF16)

    chunks(width, CHUNK, combine)

    for kind in range(5):

        @pl.loop(1, owners)
        def _(step, kind=kind):
            block_copy(kind, step).wait_send()


def body(
    activations, gradients, stashed, norm_gain, router,
    gate_weight, up_weight, down_weight, routes_forward, routes_backward,
):
    owners, sections = lax.axis_size("expert"), lax.axis_size("section")
    rows, width = activations.shape[1:]
    top = routes_forward.shape[2]
    hidden_width = gate_weight.shape[3]
    capacity = 3 * rows * top // (2 * owners)
    capacity = -(-capacity // 16) * 16
    slots = owners * capacity
    router_mat = jnp.pad(router[0], ((0, 0), (0, LANES - router.shape[2])))
    vmem, hbm = pl.BlockSpec(memory_space=pltpu.VMEM), pl.BlockSpec(memory_space=pl.ANY)
    plain, wide = pltpu.VMEM((slots, width), BF16), pltpu.VMEM((slots, width + LANES), BF16)
    inner = pltpu.VMEM((slots, hidden_width), BF16)
    inner_f32 = pltpu.VMEM((slots, hidden_width), F32)
    tokens = pltpu.VMEM((rows, width), BF16)
    layer_out, input_grad = pl.pallas_call(
        functools.partial(kernel, owners, sections, capacity, top),
        out_shape=[jax.ShapeDtypeStruct((rows, width), BF16)] * 2,
        in_specs=[vmem] * 7 + [hbm] * 3,
        out_specs=[vmem] * 2,
        scratch_shapes=[
            pltpu.VMEM((width, hidden_width), BF16),
            pltpu.VMEM((width, hidden_width), BF16),
            pltpu.VMEM((hidden_width, width), BF16),
            tokens, tokens,
            plain, wide, plain, wide, plain,
            plain, wide, plain, wide, plain,
            tokens, inner_f32, inner_f32, inner, plain, plain, inner, inner,
            pltpu.VMEM((slots, LANES), F32),
            pltpu.SemaphoreType.DMA((3,)),
            pltpu.SemaphoreType.DMA((2,)),
            pltpu.SemaphoreType.DMA((2,)),
            pltpu.SemaphoreType.DMA((5, owners)),
            pltpu.SemaphoreType.DMA((5, owners)),
        ],
        compiler_params=pltpu.CompilerParams(
            collective_id=0, has_side_effects=True, vmem_limit_bytes=58 << 20
        ),
        cost_estimate=pl.CostEstimate(
            flops=18 * slots * width * hidden_width,
            bytes_accessed=6 * width * hidden_width + 10 * rows * width,
            transcendentals=3 * slots * hidden_width,
        ),
    )(
        activations[0], gradients[0], stashed[0], norm_gain, router_mat,
        routes_forward[0], routes_backward[0],
        gate_weight[0, 0], up_weight[0, 0], down_weight[0, 0],
    )
    return layer_out[None], input_grad[None]


def solution(mesh):
    rows = P("section", "expert", None)
    experts = P("section", "expert", None, None)
    placed = (
        rows, rows, rows, P("section", None), P("section", None, None),
        experts, experts, experts, rows, rows,
    )
    return jax.shard_map(
        body, mesh=mesh, in_specs=placed, out_specs=(rows, rows), check_vma=False
    )
```

time: 176 us -> 110 us (0.62)
  the two profiles are of different devices: /device:TPU:0 before, /device:TPU:1 now
where the time goes in v1:
time: 110 us
  Pallas kernels  100 us (91%)
  local copies, waits for them, and re-layouts  8.52 us (8%)
    pallas_call x1, Pallas kernels, body(): pl.pallas_call(functools.partial(kernel, owners, sections, capacity, top)...  100 us
    unnamed x5, local copies, waits for them, and re-layouts  7.61 us

profile of v1, /device:TPU:1, one launch (start us, length us, event | category | flops | bytes accessed | tf_op | source)
XLA Modules:
  0.0 109.6 jit_solution(16752238667268944497)
XLA Ops:
  0.6 1.4 %copy.13 = s32[1,128,2]{2,1,0:T(8,128)} copy(s32[1,128,2]{1,2,0:T(2,128)} %param.18) | data formatting | bytes 2048 | tf_op args[8]
  2.0 1.4 %copy.14 = s32[1,128,2]{2,1,0:T(8,128)} copy(s32[1,128,2]{1,2,0:T(2,128)} %param.19) | data formatting | bytes 2048 | tf_op args[9]
  3.5 1.0 copy.12
  4.5 0.9 pad.4.router_ref
  5.4 100.4 %shard_map.113 = (bf16[128,2048]{1,0:T(8,128)(2,1)}, bf16[128,2048]{1,0:T(8,128)(2,1)}) custom-call(bf16[128,2048]{1,0:T(8,128)(2,1)} %bitcast.19, bf16[128,2048]{1,0:T(8,128)(2,1)} %bitcast.20, bf16[128,2048]{1,0:T(8,128)(2,1)} %bitcast.21, bf16[1,2048]{1,0:T(2,128)(2,1)} %gain_ref.1, bf16[2048,128]{1,0:T(8,128)(2,1)} %pad.4.router_ref, s32[128,2]{1,0:T(8,128)} %bitcast.14, ...), custom_call_target="tpu_custom_call" | custom-call | flops 10871635968 | bytes 12058624 | tf_op jit(solution)/shard_map/pallas_call | solution.py:312
  105.8 1.9 %copy.17 = bf16[1,128,2048]{2,1,0:T(8,128)(2,1)} copy(bf16[1,128,2048]{2,1,0:T(8,128)(2,1)} %bitcast.13) | data formatting | bytes 1048576
  107.7 1.9 %copy.18 = bf16[1,128,2048]{2,1,0:T(8,128)(2,1)} copy(bf16[1,128,2048]{2,1,0:T(8,128)(2,1)} %bitcast.12) | data formatting | bytes 1048576

commit v2 on v1

--- a/solution.py
+++ b/solution.py
@@ -37,20 +37,27 @@
 
 
 def places(routes, top, capacity):
-    rows = routes.shape[0]
-    columns = lax.broadcasted_iota(jnp.int32, (rows, LANES), 1)
-    matches = [(routes[:, k : k + 1] == columns).astype(F32) for k in range(top)]
+    rows = routes.shape[1]
+    columns = lax.broadcasted_iota(jnp.int32, (rows, LANES), 1).astype(F32)
+    across = lax.broadcasted_iota(jnp.int32, (rows, rows), 1)
+    down = lax.broadcasted_iota(jnp.int32, (rows, rows), 0)
+    named = [
+        jnp.sum(
+            jnp.where(across == down, routes[k : k + 1, :].astype(F32), 0.0),
+            axis=1, keepdims=True,
+        )
+        for k in range(top)
+    ]
+    matches = [(n == columns).astype(F32) for n in named]
     per_row = sum(matches)
-    before = lax.broadcasted_iota(jnp.int32, (rows, rows), 1) < lax.broadcasted_iota(
-        jnp.int32, (rows, rows), 0
-    )
+    before = across < down
     earlier = mm(before.astype(F32).astype(BF16), per_row.astype(BF16))
-    offsets = earlier + columns.astype(F32) * capacity
+    offsets = earlier + columns * capacity
     return matches, [jnp.sum(m * offsets, axis=1, keepdims=True) for m in matches]
 
 
 def route_weights(normed, router, matches):
-    logits = mm(normed, router)
+    logits = mm(normed, router, NT)
     sig = [jax.nn.sigmoid(jnp.sum(m * logits, axis=1, keepdims=True)) for m in matches]
     total = sum(sig)
     return [s / total for s in sig], sig, total
@@ -102,8 +109,6 @@
 
     for neighbour in (after, before):
         pl.semaphore_signal(barrier, inc=1, device_id={"section": neighbour}, device_id_type=MESH)
-    pl.semaphore_wait(barrier, owners + 1)
-
     def rows_of(index):
         return pl.ds(pl.multiple_of(index * capacity, 16), capacity)
 
@@ -147,10 +152,11 @@
 
     grad_hop = hop(0, grad_ref, cot, before)
     act_hop = hop(1, act_ref, arrived, after)
-    grad_hop.start()
-
     gain = gain_ref[...].astype(F32)
-    router = router_ref[...]
+    experts = router_ref.shape[0]
+    router = jnp.concatenate(
+        [router_ref[...].astype(F32), jnp.zeros((LANES - experts, width), F32)], axis=0
+    ).astype(BF16)
     ones = [1.0] * top
 
     match_b, pos_b = places(routes_b_ref[...], top, capacity)
@@ -163,6 +169,8 @@
         send_b[:, cols] = mm(spread_b, normed[:, cols]).astype(BF16)
 
     chunks(width, CHUNK, fill_b)
+    pl.semaphore_wait(barrier, owners + 1)
+    grad_hop.start()
     send(ROW_B)
     weights_b, sig_b, total_b = route_weights(normed[...], router, match_b)
     scales = [w.astype(BF16).astype(F32) for w in weights_b]
@@ -195,11 +203,6 @@
 
         chunks(width, CHUNK, work)
 
-    for load in loads:
-        load.wait()
-    receive(ROW_B)
-    expert_hidden(recv_b, True)
-
     match_f, pos_f = places(routes_f_ref[...], top, capacity)
     spread_f = table(pos_f, ones, slots).T.astype(BF16)
     act_hop.wait()
@@ -210,8 +213,12 @@
         send_f[:, cols] = mm(spread_f, normed[:, cols]).astype(BF16)
 
     chunks(width, CHUNK, fill_f)
+    weights_f = route_weights(normed[...], router, match_f)[0]
+    for load in loads:
+        load.wait()
+    receive(ROW_B)
     send(ROW_F)
-    weights_f = route_weights(normed[...], router, match_f)[0]
+    expert_hidden(recv_b, True)
     expert_down(out_b)
 
     receive(ROW_C)
@@ -263,8 +270,8 @@
     gather_b = table(pos_b, ones, slots).astype(BF16)
     grad_normed = (
         mm(gather_b, recv_g[:, :width])
-        + mm(logits_high, router, NT)
-        + mm(logits_low, router, NT)
+        + mm(logits_high, router)
+        + mm(logits_low, router)
     )
     grad_pre = grad_normed * gain
     values = stored_ref[...].astype(F32)
@@ -290,6 +297,11 @@
         @pl.loop(1, owners)
         def _(step, kind=kind):
             block_copy(kind, step).wait_send()
+
+
+def hand_over(layer_in, grad_in, layer_ref, input_ref):
+    layer_ref[...] = layer_in[...]
+    input_ref[...] = grad_in[...]
 
 
 def body(
@@ -303,7 +315,6 @@
     capacity = 3 * rows * top // (2 * owners)
     capacity = -(-capacity // 16) * 16
     slots = owners * capacity
-    router_mat = jnp.pad(router[0], ((0, 0), (0, LANES - router.shape[2])))
     vmem, hbm = pl.BlockSpec(memory_space=pltpu.VMEM), pl.BlockSpec(memory_space=pl.ANY)
     plain, wide = pltpu.VMEM((slots, width), BF16), pltpu.VMEM((slots, width + LANES), BF16)
     inner = pltpu.VMEM((slots, hidden_width), BF16)
@@ -338,10 +349,17 @@
             transcendentals=3 * slots * hidden_width,
         ),
     )(
-        activations[0], gradients[0], stashed[0], norm_gain, router_mat,
-        routes_forward[0], routes_backward[0],
+        activations[0], gradients[0], stashed[0], norm_gain, router[0].T,
+        routes_forward[0].T, routes_backward[0].T,
         gate_weight[0, 0], up_weight[0, 0], down_weight[0, 0],
     )
+    layer_out, input_grad = pl.pallas_call(
+        hand_over,
+        grid=(rows // 32,),
+        out_shape=[jax.ShapeDtypeStruct((rows, width), BF16)] * 2,
+        in_specs=[pl.BlockSpec((32, width), lambda i: (i, 0))] * 2,
+        out_specs=[pl.BlockSpec((32, width), lambda i: (i, 0))] * 2,
+    )(layer_out, input_grad)
     return layer_out[None], input_grad[None]
 
 

time: 110 us -> 102 us (0.927)
  local copies, waits for them, and re-layouts: 8.52 us -> 0 us
  Pallas kernels: 100 us -> 102 us
    unnamed x5 -> x0, local copies, waits for them, and re-layouts: 7.61 us -> none
    pallas_call x0 -> x1, Pallas kernels: none -> 3.41 us  [body(): pl.pallas_call(hand_over, grid=(rows // 32,), out_shape=[jax.ShapeDtypeSt...]
    pallas_call x1, Pallas kernels: 100 us -> 98.1 us  [body(): pl.pallas_call(functools.partial(kernel, owners, sections, capacity, top)...]
where the time goes in v2:
time: 102 us
  Pallas kernels  102 us (100%)
    pallas_call x1, Pallas kernels, body(): pl.pallas_call(functools.partial(kernel, owners, sections, capacity, top)...  98.1 us
    pallas_call x1, Pallas kernels, body(): pl.pallas_call(hand_over, grid=(rows // 32,), out_shape=[jax.ShapeDtypeSt...  3.41 us

profile of v2, /device:TPU:1, one launch (start us, length us, event | category | flops | bytes accessed | tf_op | source)
XLA Modules:
  0.0 102.2 jit_solution(10029180398750027683)
XLA Ops:
  0.6 98.1 %shard_map.113 = (bf16[128,2048]{1,0:T(8,128)(2,1)}, bf16[128,2048]{1,0:T(8,128)(2,1)}) custom-call(bf16[128,2048]{1,0:T(8,128)(2,1)} %bitcast.20, bf16[128,2048]{1,0:T(8,128)(2,1)} %bitcast.21, bf16[128,2048]{1,0:T(8,128)(2,1)} %bitcast.22, bf16[1,2048]{1,0:T(2,128)(2,1)} %gain_ref.1, bf16[8,2048]{1,0:T(8,128)(2,1)} %bitcast.25, s32[2,128]{1,0:T(2,128)} %bitcast.26, ...), custom_call_target="tpu_custom_call" | custom-call | flops 10871635968 | bytes 12058624 | tf_op jit(solution)/shard_map/pallas_call | solution.py:323
  98.7 3.4 %shard_map.114 = (bf16[128,2048]{1,0:T(8,128)(2,1)}, bf16[128,2048]{1,0:T(8,128)(2,1)}) custom-call(bf16[128,2048]{1,0:T(8,128)(2,1)} %get-tuple-element.6.layer_in, bf16[128,2048]{1,0:T(8,128)(2,1)} %get-tuple-element.7.grad_in), custom_call_target="tpu_custom_call" | custom-call | tf_op jit(solution)/shard_map/pallas_call | solution.py:356

commit v3 on v2

--- a/solution.py
+++ b/solution.py
@@ -26,8 +26,8 @@
     return high, (value - high.astype(F32)).astype(BF16)
 
 
-def chunks(width, step, work):
-    @pl.loop(0, width // step)
+def chunks(start, stop, step, work):
+    @pl.loop(start // step, stop // step)
     def _(index):
         work(pl.ds(pl.multiple_of(index * step, step), step))
 
@@ -112,33 +112,48 @@
     def rows_of(index):
         return pl.ds(pl.multiple_of(index * capacity, 16), capacity)
 
-    def block_copy(kind, step):
+    half = width // 2
+
+    def columns_of(kind, part):
+        stop = sends[kind].shape[1] if part else half
+        return pl.ds(part * half, stop - part * half)
+
+    def block_copy(kind, part, step):
         peer = lax.rem(me + step, owners)
+        cols = columns_of(kind, part)
         return pltpu.make_async_remote_copy(
-            src_ref=sends[kind].at[rows_of(peer)],
-            dst_ref=recvs[kind].at[rows_of(me)],
-            send_sem=send_sem.at[kind, step],
-            recv_sem=recv_sem.at[kind, step],
+            src_ref=sends[kind].at[rows_of(peer), cols],
+            dst_ref=recvs[kind].at[rows_of(me), cols],
+            send_sem=send_sem.at[2 * kind + part, step],
+            recv_sem=recv_sem.at[2 * kind + part, step],
             device_id={"expert": peer},
             device_id_type=MESH,
         )
 
-    def send(kind):
+    def send(kind, part):
         @pl.loop(1, owners)
         def _(step):
-            block_copy(kind, step).start()
-
-        recvs[kind][rows_of(me)] = sends[kind][rows_of(me)]
-
-    def receive(kind):
+            block_copy(kind, part, step).start()
+
+        cols = columns_of(kind, part)
+        recvs[kind][rows_of(me), cols] = sends[kind][rows_of(me), cols]
+
+    def fill_and_send(kind, work):
+        for part in range(2):
+            chunks(part * half, (part + 1) * half, CHUNK, work)
+            send(kind, part)
+
+    def receive(kind, part):
+        cols = columns_of(kind, part)
+
         @pl.loop(1, owners)
         def _(step):
             source = lax.rem(me + owners - step, owners)
             pltpu.make_async_remote_copy(
-                src_ref=sends[kind].at[rows_of(source)],
-                dst_ref=recvs[kind].at[rows_of(source)],
-                send_sem=send_sem.at[kind, step],
-                recv_sem=recv_sem.at[kind, step],
+                src_ref=sends[kind].at[rows_of(source), cols],
+                dst_ref=recvs[kind].at[rows_of(source), cols],
+                send_sem=send_sem.at[2 * kind + part, step],
+                recv_sem=recv_sem.at[2 * kind + part, step],
                 device_id={"expert": source},
                 device_id_type=MESH,
             ).wait_recv()
@@ -168,10 +183,12 @@
     def fill_b(cols):
         send_b[:, cols] = mm(spread_b, normed[:, cols]).astype(BF16)
 
-    chunks(width, CHUNK, fill_b)
+    chunks(0, half, CHUNK, fill_b)
     pl.semaphore_wait(barrier, owners + 1)
+    send(ROW_B, 0)
     grad_hop.start()
-    send(ROW_B)
+    chunks(half, width, CHUNK, fill_b)
+    send(ROW_B, 1)
     weights_b, sig_b, total_b = route_weights(normed[...], router, match_b)
     scales = [w.astype(BF16).astype(F32) for w in weights_b]
     scale_table = table(pos_b, scales, slots).T.astype(BF16)
@@ -183,8 +200,7 @@
     def fill_c(cols):
         send_c[:, cols] = mm(spread_b, cot[:, cols]).astype(BF16)
 
-    chunks(width, CHUNK, fill_c)
-    send(ROW_C)
+    fill_and_send(ROW_C, fill_c)
 
     def expert_hidden(rows_ref, keep):
         def work(cols):
@@ -195,13 +211,13 @@
                 upper[:, cols] = u
             hidden[:, cols] = (g * jax.nn.sigmoid(g) * u).astype(BF16)
 
-        chunks(hidden_width, CHUNK, work)
+        chunks(0, hidden_width, CHUNK, work)
 
     def expert_down(target):
         def work(cols):
             target[:, cols] = mm(hidden[...], down_w[:, cols]).astype(BF16)
 
-        chunks(width, CHUNK, work)
+        return work
 
     match_f, pos_f = places(routes_f_ref[...], top, capacity)
     spread_f = table(pos_f, ones, slots).T.astype(BF16)
@@ -212,16 +228,19 @@
     def fill_f(cols):
         send_f[:, cols] = mm(spread_f, normed[:, cols]).astype(BF16)
 
-    chunks(width, CHUNK, fill_f)
+    chunks(0, width, CHUNK, fill_f)
     weights_f = route_weights(normed[...], router, match_f)[0]
     for load in loads:
         load.wait()
-    receive(ROW_B)
-    send(ROW_F)
+    for part in range(2):
+        receive(ROW_B, part)
+    for part in range(2):
+        send(ROW_F, part)
     expert_hidden(recv_b, True)
-    expert_down(out_b)
-
-    receive(ROW_C)
+    chunks(0, width, CHUNK, expert_down(out_b))
+
+    for part in range(2):
+        receive(ROW_C, part)
     acc[...] = jnp.zeros_like(acc)
     scale = recv_c[:, width:].astype(F32)[:, :1]
 
@@ -231,7 +250,9 @@
         product = rows * out_b[:, cols].astype(F32)
         acc[...] += product[:, :LANES] + product[:, LANES:]
 
-    chunks(width, CHUNK, scale_rows)
+    chunks(0, width, CHUNK, scale_rows)
+    scores = jnp.sum(acc[...], axis=1, keepdims=True)
+    send_g[:, width:] = jnp.broadcast_to(scores, (slots, LANES)).astype(BF16)
 
     def hidden_grads(cols):
         grad_hidden = mm(slot_grad[...], down_w[cols, :], NT)
@@ -242,23 +263,21 @@
             grad_hidden * upper[:, cols] * s * (1.0 + g * (1.0 - s))
         ).astype(BF16)
 
-    chunks(hidden_width, CHUNK, hidden_grads)
+    chunks(0, hidden_width, CHUNK, hidden_grads)
 
     def row_grads(cols):
         total = mm(grad_gate[...], gate_w[cols, :], NT) + mm(grad_up[...], up_w[cols, :], NT)
         send_g[:, cols] = total.astype(BF16)
 
-    chunks(width, CHUNK, row_grads)
-    scores = jnp.sum(acc[...], axis=1, keepdims=True)
-    send_g[:, width:] = jnp.broadcast_to(scores, (slots, LANES)).astype(BF16)
-    send(OUT_G)
-
-    receive(ROW_F)
+    fill_and_send(OUT_G, row_grads)
+
+    for part in range(2):
+        receive(ROW_F, part)
     expert_hidden(recv_f, False)
-    expert_down(send_o)
-    send(OUT_F)
-
-    receive(OUT_G)
+    fill_and_send(OUT_F, expert_down(send_o))
+
+    for part in range(2):
+        receive(OUT_G, part)
     score = [
         mm(table([p], [1.0], slots).astype(BF16), recv_g[:, width:])[:, :1] for p in pos_b
     ]
@@ -283,25 +302,38 @@
     ).astype(BF16)
 
     weight_high, weight_low = halves(table(pos_f, weights_f, slots))
-    receive(OUT_F)
 
     def combine(cols):
         rows = recv_o[:, cols]
         mixed_rows = mm(weight_high, rows) + mm(weight_low, rows)
         layer_ref[:, cols] = (arrived[:, cols].astype(F32) + mixed_rows).astype(BF16)
 
-    chunks(width, CHUNK, combine)
+    for part in range(2):
+        receive(OUT_F, part)
+        chunks(part * half, (part + 1) * half, CHUNK, combine)
 
     for kind in range(5):
-
-        @pl.loop(1, owners)
-        def _(step, kind=kind):
-            block_copy(kind, step).wait_send()
-
-
-def hand_over(layer_in, grad_in, layer_ref, input_ref):
-    layer_ref[...] = layer_in[...]
-    input_ref[...] = grad_in[...]
+        for part in range(2):
+
+            @pl.loop(1, owners)
+            def _(step, kind=kind, part=part):
+                block_copy(kind, part, step).wait_send()
+
+
+def hand_over(layer_in, grad_in, layer_ref, input_ref, sem):
+    count = sem.shape[1]
+    share = layer_in.shape[0] // count
+    copies = [
+        pltpu.make_async_copy(
+            source.at[pl.ds(i * share, share)], target.at[pl.ds(i * share, share)], sem.at[j, i]
+        )
+        for j, (source, target) in enumerate(((layer_in, layer_ref), (grad_in, input_ref)))
+        for i in range(count)
+    ]
+    for copy in copies:
+        copy.start()
+    for copy in copies:
+        copy.wait()
 
 
 def body(
@@ -337,8 +369,8 @@
             pltpu.SemaphoreType.DMA((3,)),
             pltpu.SemaphoreType.DMA((2,)),
             pltpu.SemaphoreType.DMA((2,)),
-            pltpu.SemaphoreType.DMA((5, owners)),
-            pltpu.SemaphoreType.DMA((5, owners)),
+            pltpu.SemaphoreType.DMA((10, owners)),
+            pltpu.SemaphoreType.DMA((10, owners)),
         ],
         compiler_params=pltpu.CompilerParams(
             collective_id=0, has_side_effects=True, vmem_limit_bytes=58 << 20
@@ -355,10 +387,10 @@
     )
     layer_out, input_grad = pl.pallas_call(
         hand_over,
-        grid=(rows // 32,),
         out_shape=[jax.ShapeDtypeStruct((rows, width), BF16)] * 2,
-        in_specs=[pl.BlockSpec((32, width), lambda i: (i, 0))] * 2,
-        out_specs=[pl.BlockSpec((32, width), lambda i: (i, 0))] * 2,
+        in_specs=[hbm] * 2,
+        out_specs=[hbm] * 2,
+        scratch_shapes=[pltpu.SemaphoreType.DMA((2, 4))],
     )(layer_out, input_grad)
     return layer_out[None], input_grad[None]
 

time: 102 us -> 132 us (1.29)
  Pallas kernels: 102 us -> 131 us
    pallas_call x1, Pallas kernels: 3.41 us -> 32.9 us  [body(): pl.pallas_call(hand_over, out_shape=[jax.ShapeDtypeStruct((rows, width),...]
where the time goes in v3:
time: 132 us
  Pallas kernels  131 us (99%)
    pallas_call x1, Pallas kernels, body(): pl.pallas_call(functools.partial(kernel, owners, sections, capacity, top)...  98.4 us
    pallas_call x1, Pallas kernels, body(): pl.pallas_call(hand_over, out_shape=[jax.ShapeDtypeStruct((rows, width),...  32.9 us

profile of v3, /device:TPU:1, one launch (start us, length us, event | category | flops | bytes accessed | tf_op | source)
XLA Modules:
  0.0 132.0 jit_solution(18199887813431905772)
XLA Ops:
  0.6 98.4 %shard_map.113 = (bf16[128,2048]{1,0:T(8,128)(2,1)}, bf16[128,2048]{1,0:T(8,128)(2,1)}) custom-call(bf16[128,2048]{1,0:T(8,128)(2,1)} %bitcast.20, bf16[128,2048]{1,0:T(8,128)(2,1)} %bitcast.21, bf16[128,2048]{1,0:T(8,128)(2,1)} %bitcast.22, bf16[1,2048]{1,0:T(2,128)(2,1)} %gain_ref.1, bf16[8,2048]{1,0:T(8,128)(2,1)} %bitcast.25, s32[2,128]{1,0:T(2,128)} %bitcast.26, ...), custom_call_target="tpu_custom_call" | custom-call | flops 10871635968 | bytes 12058624 | tf_op jit(solution)/shard_map/pallas_call | solution.py:355
  99.0 32.9 %shard_map.114 = (bf16[128,2048]{1,0:T(8,128)(2,1)}, bf16[128,2048]{1,0:T(8,128)(2,1)}) custom-call(bf16[128,2048]{1,0:T(8,128)(2,1)} %get-tuple-element.6.layer_in, bf16[128,2048]{1,0:T(8,128)(2,1)} %get-tuple-element.7.grad_in), custom_call_target="tpu_custom_call" | custom-call | tf_op jit(solution)/shard_map/pallas_call | solution.py:388

commit v4 on v2

--- a/solution.py
+++ b/solution.py
@@ -216,8 +216,8 @@
     weights_f = route_weights(normed[...], router, match_f)[0]
     for load in loads:
         load.wait()
+    send(ROW_F)
     receive(ROW_B)
-    send(ROW_F)
     expert_hidden(recv_b, True)
     expert_down(out_b)
 
@@ -355,10 +355,9 @@
     )
     layer_out, input_grad = pl.pallas_call(
         hand_over,
-        grid=(rows // 32,),
         out_shape=[jax.ShapeDtypeStruct((rows, width), BF16)] * 2,
-        in_specs=[pl.BlockSpec((32, width), lambda i: (i, 0))] * 2,
-        out_specs=[pl.BlockSpec((32, width), lambda i: (i, 0))] * 2,
+        in_specs=[vmem] * 2,
+        out_specs=[vmem] * 2,
     )(layer_out, input_grad)
     return layer_out[None], input_grad[None]
 

time: 102 us -> 101 us (level)
  Pallas kernels: 102 us -> 100 us
    pallas_call x1, Pallas kernels: 3.41 us -> 2.2 us  [body(): pl.pallas_call(hand_over, out_shape=[jax.ShapeDtypeStruct((rows, width),...]
where the time goes in v4:
time: 101 us
  Pallas kernels  100 us (99%)
    pallas_call x1, Pallas kernels, body(): pl.pallas_call(functools.partial(kernel, owners, sections, capacity, top)...  98.1 us
    pallas_call x1, Pallas kernels, body(): pl.pallas_call(hand_over, out_shape=[jax.ShapeDtypeStruct((rows, width),...  2.2 us

profile of v4, /device:TPU:1, one launch (start us, length us, event | category | flops | bytes accessed | tf_op | source)
XLA Modules:
  0.0 101.0 jit_solution(17328612249919155106)
XLA Ops:
  0.6 98.1 %shard_map.113 = (bf16[128,2048]{1,0:T(8,128)(2,1)}, bf16[128,2048]{1,0:T(8,128)(2,1)}) custom-call(bf16[128,2048]{1,0:T(8,128)(2,1)} %bitcast.20, bf16[128,2048]{1,0:T(8,128)(2,1)} %bitcast.21, bf16[128,2048]{1,0:T(8,128)(2,1)} %bitcast.22, bf16[1,2048]{1,0:T(2,128)(2,1)} %gain_ref.1, bf16[8,2048]{1,0:T(8,128)(2,1)} %bitcast.25, s32[2,128]{1,0:T(2,128)} %bitcast.26, ...), custom_call_target="tpu_custom_call" | custom-call | flops 10871635968 | bytes 12058624 | tf_op jit(solution)/shard_map/pallas_call | solution.py:323
  98.7 2.2 %shard_map.114 = (bf16[128,2048]{1,0:T(8,128)(2,1)}, bf16[128,2048]{1,0:T(8,128)(2,1)}) custom-call(bf16[128,2048]{1,0:T(8,128)(2,1)} %get-tuple-element.6.layer_in, bf16[128,2048]{1,0:T(8,128)(2,1)} %get-tuple-element.7.grad_in), custom_call_target="tpu_custom_call" | custom-call | tf_op jit(solution)/shard_map/pallas_call | solution.py:356
